TPU v7x, 32 devices: a whole 2x2x4 slice. The times are simulated.
32 devices in a mesh: seq: 8 (over z, y), chan: 4 (over x, core).
Axes of the slice: x: 2, y: 2, z: 4, core: 2. Of those that a mesh axis runs over, the one named last changes fastest.
Arguments:
- inputs: bfloat16 [2, 8192, 2048], P(None, 'seq', 'chan'), may hold values from -6 to 6
- mix_first: bfloat16 [32, 256, 256], P('seq'), may hold values from -0.375 to 0.375
- mix_second: bfloat16 [256, 32, 32], P('seq'), may hold values from -1 to 1
- gate_scale: float32 [2048], P('chan'), may hold values from 0.5 to 2
- gate_bias: float32 [2048], P('chan'), may hold values from -3 to 3
- up_first: bfloat16 [4, 512, 512], P('chan'), may hold values from -0.25 to 0.25
- up_second: bfloat16 [4, 2048, 512], P('chan'), may hold values from -0.25 to 0.25
- down_first: bfloat16 [4, 512, 2048], P('chan'), may hold values from -0.125 to 0.125
- down_second: bfloat16 [4, 512, 512], P('chan'), may hold values from -0.25 to 0.25
Outputs:
- layer_out: bfloat16 [2, 8192, 2048], P(None, ('seq', 'chan'))
All inputs are finite; a program needn't handle non-finite values.
Results may differ from a plain program's by a relative error of at most 0.008.
Values may be sent and summed in bfloat16 or wider, within the bound.
A program may use at most 128 MiB of HBM per device.

v0:
```python
import jax
import jax.numpy as jnp
from jax import lax
from jax.sharding import PartitionSpec as P


def shard_monarch(values, inner_weight, outer_weight):
    chan_count = lax.axis_size("chan")
    inner_width = inner_weight.shape[1]
    out_width = outer_weight.shape[1]
    sub_width = inner_width // chan_count
    seq_count, row_count = (values.shape[0], values.shape[1])
    inner_rows = jnp.einsum(
        "qp,stp->stq", inner_weight[0], values, preferred_element_type=jnp.float32
    )
    inner_rows = inner_rows.astype(jnp.bfloat16).reshape(
        seq_count, row_count, chan_count, sub_width
    )
    permuted = lax.all_to_all(inner_rows, "chan", split_axis=2, concat_axis=2, tiled=True)
    outer_blocks = outer_weight[0].reshape(out_width, sub_width, chan_count)
    return jnp.einsum("oqc,stcq->sto", outer_blocks, permuted, preferred_element_type=jnp.float32)


def on_device(
    inputs,
    mix_first,
    mix_second,
    gate_scale,
    gate_bias,
    up_first,
    up_second,
    down_first,
    down_second,
):
    seq_count, row_count, chan_width = inputs.shape
    blocks_here = mix_first.shape[0]
    group_width = mix_first.shape[1]
    grouped = inputs.reshape(seq_count, blocks_here, group_width, chan_width)
    first_pass = jnp.einsum(
        "abq,saqc->sabc", mix_first, grouped, preferred_element_type=jnp.float32
    ).astype(jnp.bfloat16)
    mixed_rows = jnp.einsum(
        "bxy,sybc->sxbc",
        mix_second,
        lax.all_to_all(first_pass, "seq", split_axis=2, concat_axis=1, tiled=True),
        preferred_element_type=jnp.float32,
    ).astype(jnp.bfloat16)
    restored = lax.all_to_all(mixed_rows, "seq", split_axis=1, concat_axis=2, tiled=True).reshape(
        seq_count, row_count, chan_width
    )
    residual_in = inputs.astype(jnp.float32)
    hidden = (
        residual_in
        + restored.astype(jnp.float32) * jax.nn.sigmoid(gate_scale * residual_in + gate_bias)
    ).astype(jnp.bfloat16)
    expanded = shard_monarch(hidden, up_first, up_second)
    activated = jax.nn.gelu(expanded, approximate=True).astype(jnp.bfloat16)
    contracted = shard_monarch(activated, down_first, down_second)
    result = (hidden.astype(jnp.float32) + contracted).astype(jnp.bfloat16)
    return lax.all_to_all(result, "chan", split_axis=1, concat_axis=2, tiled=True)


def solution(mesh):
    return jax.shard_map(
        on_device,
        mesh=mesh,
        in_specs=(
            P(None, "seq", "chan"),
            P("seq", None, None),
            P("seq", None, None),
            P("chan"),
            P("chan"),
            P("chan", None, None),
            P("chan", None, None),
            P("chan", None, None),
            P("chan", None, None),
        ),
        out_specs=P(None, ("seq", "chan"), None),
        check_vma=False,
    )
```

profile of v0, /device:TPU:29, one launch (start us, length us, event | category | flops | bytes accessed | tf_op | source)
XLA Modules:
  0.0 255.7 jit_solution(4681030147470669470)
XLA Ops:
  0.0 4.1 %convert_bitcast_fusion.1 = bf16[2,4,256,512]{2,3,0,1:T(8,128)(2,1)} fusion(bf16[2,4,256,512]{3,2,1,0:T(8,128)(2,1)} %bitcast.65, bf16[4,256,256]{2,1,0:T(8,128)(2,1)} %param.10), kind=kOutput, calls=%fused_computation.27 | convolution fusion | flops 537919488 | bytes 4718592 | tf_op jit(solution)/shard_map/abq,saqc->sabc/dot_general | solution.py:39
  4.1 6.2 %copy.30 = bf16[2,4,256,512]{3,0,1,2:T(2,128)(2,1)} copy(bf16[2,4,256,512]{2,3,0,1:T(8,128)(2,1)} %convert_bitcast_fusion.1) | data formatting | bytes 4194304 | tf_op jit(solution)/shard_map/convert_element_type | solution.py:41
  10.3 51.5 %all_to_all.55 = bf16[2,4,256,512]{3,0,1,2:T(2,128)(2,1)S(1)} all-to-all(bf16[2,4,256,512]{3,0,1,2:T(2,128)(2,1)} %copy.30), channel_id=1, replica_groups=mesh['seq'=8,'chan'=4] {'seq'}, dimensions={2} | all-to-all | bytes 4194304 | tf_op jit(solution)/shard_map/all_to_all | solution.py:45
  62.4 2.9 %copy.32 = bf16[2,8,4,32,512]{4,2,1,0,3:T(4,128)(2,1)} copy(bf16[2,8,4,32,512]{4,3,1,2,0:T(8,128)(2,1)S(1)} %bitcast.63) | data formatting | bytes 4194304 | tf_op jit(solution)/shard_map/all_to_all | solution.py:45
  65.4 4.0 %all_to_all.42 = bf16[2,32,32,512]{3,1,0,2:T(8,128)(2,1)} reshape(bf16[2,8,4,32,512]{4,2,1,0,3:T(4,128)(2,1)} %copy.32) | data formatting | bytes 4194304 | tf_op jit(solution)/shard_map/all_to_all | solution.py:45
  69.4 2.3 convert_bitcast_fusion
  71.7 2.2 copy.33
  73.8 51.2 %all_to_all.56 = bf16[2,32,32,512]{3,0,2,1:T(2,128)(2,1)S(1)} all-to-all(bf16[2,32,32,512]{3,0,2,1:T(2,128)(2,1)S(1)} %copy.33), channel_id=1, replica_groups=mesh['seq'=8,'chan'=4] {'seq'}, dimensions={1} | all-to-all | bytes 4194304 | tf_op jit(solution)/shard_map/all_to_all | solution.py:48
  126.6 1.4 fusion.17
  128.1 2.6 %convolution_convert_fusion = bf16[2,1024,512]{1,2,0:T(8,128)(2,1)} fusion(bf16[2,1024,512]{2,1,0:T(8,128)(2,1)S(1)} %fusion.17, bf16[1,512,512]{2,1,0:T(8,128)(2,1)S(1)} %copy-done.7), kind=kOutput, calls=%fused_computation.29 | convolution fusion | flops 1074790400 | bytes 4718592 | tf_op jit(solution)/shard_map/qp,stp->stq/dot_general | solution.py:13
  130.7 3.9 %copy.35 = bf16[2,1024,4,128]{3,1,0,2:T(8,128)(2,1)} copy(bf16[2,1024,4,128]{1,3,2,0:T(8,128)(2,1)} %bitcast.68) | data formatting | bytes 4194304 | tf_op jit(solution)/shard_map/reshape | solution.py:16
  134.6 5.5 %all-to-all-start.2 = ((bf16[2,1024,4,128]{3,1,0,2:T(8,128)(2,1)}), bf16[2,1024,4,128]{3,1,0,2:T(8,128)(2,1)}, u32[]{:S(2)}, u32[]{:S(2)}) async-start(bf16[2,1024,4,128]{3,1,0,2:T(8,128)(2,1)} %copy.35), calls=%async_computation.2 | async-start | bytes 4194304 | tf_op jit(solution)/shard_map/all_to_all | solution.py:19
  140.2 4.0 %copy.36 = bf16[1,2048,512]{1,2,0:T(8,128)(2,1)} copy(bf16[1,2048,512]{2,1,0:T(8,128)(2,1)} %param.15) | data formatting | bytes 4194304 | tf_op args[6]
  144.1 4.1 %reshape_squeeze.6 = bf16[2048,128,4]{0,2,1:T(4,128)(2,1)} reshape(bf16[1,2048,512]{1,2,0:T(8,128)(2,1)} %copy.36) | data formatting | bytes 4194304 | tf_op jit(solution)/shard_map/reshape;squeeze | solution.py:20
  148.2 16.9 %all-to-all-done.2 = bf16[2,1024,4,128]{3,1,0,2:T(8,128)(2,1)} async-done(((bf16[2,1024,4,128]{3,1,0,2:T(8,128)(2,1)}), bf16[2,1024,4,128]{3,1,0,2:T(8,128)(2,1)}, u32[]{:S(2)}, u32[]{:S(2)}) %all-to-all-start.2) | async-done | bytes 2097184 | tf_op jit(solution)/shard_map/all_to_all | solution.py:19
  165.1 15.2 %fusion.25 = bf16[2,1024,512]{1,2,0:T(8,128)(2,1)} fusion(bf16[1,512,2048]{2,1,0:T(8,128)(2,1)S(1)} %copy-done, bf16[2,1024,4,128]{3,1,0,2:T(8,128)(2,1)} %all-to-all-done.2, bf16[2048,128,4,1]{0,2,1,3:T(4,128)(2,1)} %bitcast.66), kind=kOutput, calls=%fused_computation.28 | convolution fusion | flops 8628731904 | bytes 8388608 | tf_op jit(solution)/shard_map/qp,stp->stq/dot_general | solution.py:13
  180.3 4.0 %copy.39 = bf16[2,1024,4,128]{3,1,0,2:T(8,128)(2,1)} copy(bf16[2,1024,4,128]{1,3,2,0:T(8,128)(2,1)} %bitcast.67) | data formatting | bytes 4194304 | tf_op jit(solution)/shard_map/reshape | solution.py:16
  184.3 5.4 %all-to-all-start.3 = ((bf16[2,1024,4,128]{3,1,0,2:T(8,128)(2,1)}), bf16[2,1024,4,128]{3,1,0,2:T(8,128)(2,1)}, u32[]{:S(2)}, u32[]{:S(2)}) async-start(bf16[2,1024,4,128]{3,1,0,2:T(8,128)(2,1)} %copy.39), calls=%async_computation.3 | async-start | bytes 4194304 | tf_op jit(solution)/shard_map/all_to_all | solution.py:19
  190.0 24.6 %all-to-all-done.3 = bf16[2,1024,4,128]{3,1,0,2:T(8,128)(2,1)} async-done(((bf16[2,1024,4,128]{3,1,0,2:T(8,128)(2,1)}), bf16[2,1024,4,128]{3,1,0,2:T(8,128)(2,1)}, u32[]{:S(2)}, u32[]{:S(2)}) %all-to-all-start.3) | async-done | bytes 2097184 | tf_op jit(solution)/shard_map/all_to_all | solution.py:19
  214.6 3.5 %fusion.16 = bf16[2,1024,512]{2,1,0:T(8,128)(2,1)S(1)} fusion(bf16[2,1024,512]{2,1,0:T(8,128)(2,1)} %copy-done.2, bf16[2,1024,4,128]{3,1,0,2:T(8,128)(2,1)} %all-to-all-done.3, bf16[512,128,4,1]{0,2,1,3:T(4,128)(2,1)S(1)} %bitcast.69), kind=kOutput, calls=%fused_computation.19 | convolution fusion | flops 1076887552 | bytes 6815744 | tf_op jit(solution)/shard_map/oqc,stcq->sto/dot_general | solution.py:21
  218.1 2.2 copy.43
  220.3 28.0 %all_to_all.57 = bf16[2,1024,512]{2,0,1:T(2,128)(2,1)S(1)} all-to-all(bf16[2,1024,512]{2,0,1:T(2,128)(2,1)S(1)} %copy.43), channel_id=1, replica_groups=mesh['seq'=8,'chan'=4] {'chan'}, dimensions={1} | all-to-all | bytes 4194304 | tf_op jit(solution)/shard_map/all_to_all | solution.py:60
  248.3 2.9 %copy.44 = bf16[2,256,4,512]{3,2,1,0:T(4,128)(2,1)} copy(bf16[2,256,4,512]{3,0,1,2:T(2,128)(2,1)S(1)} %bitcast.64) | data formatting | bytes 4194304 | tf_op jit(solution)/shard_map/all_to_all | solution.py:60
  251.2 4.4 %all_to_all.49 = bf16[2,256,2048]{2,1,0:T(8,128)(2,1)} reshape(bf16[2,256,4,512]{3,2,1,0:T(4,128)(2,1)} %copy.44) | data formatting | bytes 4194304 | tf_op jit(solution)/shard_map/all_to_all | solution.py:60
  (20 shorter events, 2.6 us)
Async XLA Ops:
  0.0 165.1 %copy-start = (bf16[1,512,2048]{2,1,0:T(8,128)(2,1)S(1)}, bf16[1,512,2048]{2,1,0:T(8,128)(2,1)}, u32[]{:S(2)}) copy-start(bf16[1,512,2048]{2,1,0:T(8,128)(2,1)} %param.16) | copy-start | bytes 6291460
  65.4 4.0 %copy-start.4 = (bf16[32,32,32]{2,1,0:T(8,128)(2,1)S(1)}, bf16[32,32,32]{2,1,0:T(8,128)(2,1)}, u32[]{:S(2)}) copy-start(bf16[32,32,32]{2,1,0:T(8,128)(2,1)} %param.11) | copy-start | bytes 196612
  125.0 1.6 copy-start.1
  125.0 1.6 copy-start.5
  125.0 1.6 copy-start.6
  126.6 1.4 copy-start.7
  128.1 2.6 %copy-start.2 = (bf16[2,1024,512]{2,1,0:T(8,128)(2,1)}, bf16[2,1024,512]{2,1,0:T(8,128)(2,1)S(1)}, u32[]{:S(2)}) copy-start(bf16[2,1024,512]{2,1,0:T(8,128)(2,1)S(1)} %fusion.17) | copy-start | bytes 6291460
  134.6 30.5 %all-to-all-start.2 = ((bf16[2,1024,4,128]{3,1,0,2:T(8,128)(2,1)}), bf16[2,1024,4,128]{3,1,0,2:T(8,128)(2,1)}, u32[]{:S(2)}, u32[]{:S(2)}) async-start(bf16[2,1024,4,128]{3,1,0,2:T(8,128)(2,1)} %copy.35), calls=%async_computation.2 | async-start | bytes 4194304 | tf_op jit(solution)/shard_map/all_to_all | solution.py:19
  184.3 5.4 %copy-start.3 = (bf16[1,512,512]{2,1,0:T(8,128)(2,1)S(1)}, bf16[1,512,512]{2,1,0:T(8,128)(2,1)}, u32[]{:S(2)}) copy-start(bf16[1,512,512]{2,1,0:T(8,128)(2,1)} %param.17) | copy-start | bytes 1572868
  184.3 30.3 %all-to-all-start.3 = ((bf16[2,1024,4,128]{3,1,0,2:T(8,128)(2,1)}), bf16[2,1024,4,128]{3,1,0,2:T(8,128)(2,1)}, u32[]{:S(2)}, u32[]{:S(2)}) async-start(bf16[2,1024,4,128]{3,1,0,2:T(8,128)(2,1)} %copy.39), calls=%async_computation.3 | async-start | bytes 4194304 | tf_op jit(solution)/shard_map/all_to_all | solution.py:19
where the time goes:
time: 261 us; the launch traced here: 256 us
  blocking collectives  131 us (50%)
  local copies, waits for them, and re-layouts  43.4 us (17%)
  waiting for transfers between devices  41.5 us (16%)
  matrix products  27.7 us (11%)
  starting transfers between devices  10.9 us (4%)
    all_to_all x1, blocking collectives, on_device(): lax.all_to_all(first_pass, 'seq', split_axis=2, concat_axis=1, tiled=True)  51.5 us
    all_to_all x1, blocking collectives, on_device(): lax.all_to_all(mixed_rows, 'seq', split_axis=1, concat_axis=2, tiled=True)  51.2 us
    all_to_all x2, waiting for transfers between devices, shard_monarch(): lax.all_to_all(inner_rows, 'chan', split_axis=2, concat_axis=2, tiled=True)  41.5 us
    all_to_all x1, blocking collectives, on_device(): lax.all_to_all(result, 'chan', split_axis=1, concat_axis=2, tiled=True)  28 us
    dot_general x2, matrix products, shard_monarch(): jnp.einsum('qp,stp->stq', inner_weight[0], values, preferred_element_type...  17.8 us
    all_to_all x2, starting transfers between devices, shard_monarch(): lax.all_to_all(inner_rows, 'chan', split_axis=2, concat_axis=2, tiled=True)  10.9 us
    reshape x2, local copies, waits for them, and re-layouts, shard_monarch(): inner_rows.astype(jnp.bfloat16)  7.9 us
    all_to_all x3, local copies, waits for them, and re-layouts, on_device(): lax.all_to_all(first_pass, 'seq', split_axis=2, concat_axis=1, tiled=True)  7.6 us
  transfers between devices with their start and end apart: 2, of which 2 were waited for; matrix products, arithmetic and copies ran while one was open for 3% of the time, Pallas kernels for 0%

commit v1 on v0

--- a/solution.py
+++ b/solution.py
@@ -1,7 +1,14 @@
+import functools
+
 import jax
 import jax.numpy as jnp
 from jax import lax
+from jax.experimental import pallas as pl
+from jax.experimental.pallas import tpu as pltpu
 from jax.sharding import PartitionSpec as P
+
+MESH = pl.DeviceIdType.MESH
+ROWS = 16
 
 
 def shard_monarch(values, inner_weight, outer_weight):
@@ -21,7 +28,322 @@
     return jnp.einsum("oqc,stcq->sto", outer_blocks, permuted, preferred_element_type=jnp.float32)
 
 
-def on_device(
+def dot(a, b):
+    return jnp.dot(a, b, preferred_element_type=jnp.float32)
+
+
+def dot_t(a, b):
+    return lax.dot_general(a, b, (((1,), (1,)), ((), ())), preferred_element_type=jnp.float32)
+
+
+def layer_kernel(
+    n_seq,
+    n_chan,
+    x_ref,
+    mix1_ref,
+    mix2_ref,
+    scale_ref,
+    bias_ref,
+    up1_ref,
+    up2_ref,
+    down1_ref,
+    down2_ref,
+    out_ref,
+    first,
+    gathered,
+    second,
+    mixed,
+    hidden,
+    inner1,
+    perm1,
+    inner2,
+    perm2,
+    result,
+    up2p,
+    down2p,
+    spread,
+    acc,
+    fwd_send,
+    fwd_recv,
+    ret_send,
+    ret_recv,
+    c1_send,
+    c1_recv,
+    c2_send,
+    c2_recv,
+    out_send,
+    out_recv,
+    out_local,
+):
+    seqs, blocks, group, width = x_ref.shape
+    na = n_seq * blocks
+    own_b = group // n_seq
+    sub = width // n_chan
+    units = seqs * blocks
+    me_s = lax.axis_index("seq")
+    me_c = lax.axis_index("chan")
+
+    barrier = pltpu.get_barrier_semaphore()
+    for i in range(1, n_seq):
+        pl.semaphore_signal(
+            barrier, inc=1, device_id={"seq": lax.rem(me_s + i, n_seq)}, device_id_type=MESH
+        )
+    for i in range(1, n_chan):
+        pl.semaphore_signal(
+            barrier, inc=1, device_id={"chan": lax.rem(me_c + i, n_chan)}, device_id_type=MESH
+        )
+    pl.semaphore_wait(barrier, n_seq + n_chan - 2)
+
+    my_b = pl.ds(pl.multiple_of(me_s * own_b, own_b), own_b)
+    my_a = pl.ds(me_s * blocks, blocks)
+    my_sub = pl.ds(pl.multiple_of(me_c * sub, sub), sub)
+    my_cols = pl.ds(pl.multiple_of(me_c * width, width), width)
+
+    def unit_of(k):
+        j = lax.rem(k, blocks)
+        half = blocks // 2
+        return lax.div(k, blocks), lax.rem(j, 2) * half + lax.div(j, 2)
+
+    @pl.loop(0, seqs)
+    def _(s):
+        @pl.loop(0, blocks)
+        def _(a):
+            first[s, a] = dot(mix1_ref[a], x_ref[s, a]).astype(jnp.bfloat16)
+
+        @pl.loop(1, n_seq)
+        def _(i):
+            other = lax.rem(me_s + i, n_seq)
+            rows = pl.ds(pl.multiple_of(other * own_b, own_b), own_b)
+            pltpu.make_async_remote_copy(
+                src_ref=first.at[s, :, rows, :],
+                dst_ref=gathered.at[s, my_a],
+                send_sem=fwd_send.at[s],
+                recv_sem=fwd_recv.at[s],
+                device_id={"seq": other},
+                device_id_type=MESH,
+            ).start()
+
+        gathered[s, my_a] = first[s, :, my_b, :]
+
+    span = na * ROWS
+    row = lax.broadcasted_iota(jnp.int32, (width, width), 0)
+    col = lax.broadcasted_iota(jnp.int32, (width, width), 1)
+    order = (col == (row % sub) * n_chan + row // sub).astype(jnp.float32).astype(jnp.bfloat16)
+
+    @pl.loop(0, up2_ref.shape[0] // width)
+    def _(t):
+        rows = pl.ds(pl.multiple_of(t * width, width), width)
+        up2p[rows, :] = dot_t(up2_ref[rows, :], order).astype(jnp.bfloat16)
+
+    down2p[...] = dot_t(down2_ref[...], order).astype(jnp.bfloat16)
+
+    e_row = lax.broadcasted_iota(jnp.int32, (na, span), 0)
+    e_col = lax.broadcasted_iota(jnp.int32, (na, span), 1)
+    expand = (e_col // ROWS == e_row).astype(jnp.float32).astype(jnp.bfloat16)
+    s_row = lax.broadcasted_iota(jnp.int32, (span, span), 0)
+    s_col = lax.broadcasted_iota(jnp.int32, (span, span), 1)
+
+    @pl.loop(0, own_b // ROWS)
+    def _(g):
+        wide = dot(mix2_ref[g], expand)
+        spread[g] = jnp.where(s_row % ROWS == s_col % ROWS, wide, 0.0).astype(jnp.bfloat16)
+
+    @pl.loop(0, seqs)
+    def _(s):
+        others = gathered.at[s, pl.ds(0, na - blocks)]
+        pltpu.make_async_copy(others, others, fwd_recv.at[s]).wait()
+        for g in range(own_b // ROWS):
+            part = gathered[s, :, g * ROWS : (g + 1) * ROWS, :].reshape(span, width)
+            got = dot(spread[g], part).astype(jnp.bfloat16)
+            second[s, :, g * ROWS : (g + 1) * ROWS, :] = got.reshape(na, ROWS, width)
+
+        @pl.loop(0, blocks)
+        def _(j):
+            k = s * blocks + j
+            _, a = unit_of(k)
+
+            @pl.loop(1, n_seq)
+            def _(i):
+                other = lax.rem(me_s + i, n_seq)
+                pltpu.make_async_remote_copy(
+                    src_ref=second.at[s, other * blocks + a],
+                    dst_ref=mixed.at[k, my_b, :],
+                    send_sem=ret_send.at[s],
+                    recv_sem=ret_recv.at[k],
+                    device_id={"seq": other},
+                    device_id_type=MESH,
+                ).start()
+
+            mixed[k, my_b, :] = second[s, me_s * blocks + a]
+
+    def swap(k, src, dst, send_sem, recv_sem):
+        @pl.loop(1, n_chan)
+        def _(i):
+            other = lax.rem(me_c + i, n_chan)
+            cols = pl.ds(pl.multiple_of(other * sub, sub), sub)
+            pltpu.make_async_remote_copy(
+                src_ref=src.at[k, :, cols],
+                dst_ref=dst.at[k, :, my_sub],
+                send_sem=send_sem.at[k],
+                recv_sem=recv_sem.at[k],
+                device_id={"chan": other},
+                device_id_type=MESH,
+            ).start()
+
+        dst[k, :, my_sub] = src[k, :, my_sub]
+
+    def await_swap(k, dst, sem):
+        others = dst.at[k, :, pl.ds(0, width - sub)]
+        pltpu.make_async_copy(others, others, sem.at[k]).wait()
+
+    @pl.loop(0, units + 2)
+    def _(step):
+        @pl.when(step < units)
+        def _():
+            k = step
+            s, a = unit_of(k)
+            others = mixed.at[k, pl.ds(0, group - own_b), :]
+            pltpu.make_async_copy(others, others, ret_recv.at[k]).wait()
+            x = x_ref[s, a].astype(jnp.float32)
+            gate = jax.nn.sigmoid(scale_ref[...] * x + bias_ref[...])
+            hidden[k] = (x + mixed[k].astype(jnp.float32) * gate).astype(jnp.bfloat16)
+            inner1[k] = dot_t(hidden[k], up1_ref[...]).astype(jnp.bfloat16)
+            swap(k, inner1, perm1, c1_send, c1_recv)
+
+        @pl.when((step >= 1) & (step < units + 1))
+        def _():
+            k = step - 1
+            await_swap(k, perm1, c1_recv)
+            acc[...] = jnp.zeros_like(acc)
+
+            @pl.loop(0, up2_ref.shape[0] // width)
+            def _(t):
+                tile = pl.ds(pl.multiple_of(t * width, width), width)
+                act = jax.nn.gelu(dot_t(perm1[k], up2p[tile, :]), approximate=True)
+                acc[...] += dot_t(act.astype(jnp.bfloat16), down1_ref[:, tile])
+
+            inner2[k] = acc[...].astype(jnp.bfloat16)
+            swap(k, inner2, perm2, c2_send, c2_recv)
+
+        @pl.when(step >= 2)
+        def _():
+            k = step - 2
+            s, a = unit_of(k)
+            await_swap(k, perm2, c2_recv)
+            got = dot_t(perm2[k], down2p[...])
+            result[k] = (hidden[k].astype(jnp.float32) + got).astype(jnp.bfloat16)
+
+            @pl.when(a == me_c)
+            def _():
+                pltpu.make_async_copy(
+                    result.at[k], out_ref.at[s, :, my_cols], out_local.at[s]
+                ).start()
+
+            @pl.when(a != me_c)
+            def _():
+                pltpu.make_async_remote_copy(
+                    src_ref=result.at[k],
+                    dst_ref=out_ref.at[s, :, my_cols],
+                    send_sem=out_send.at[s],
+                    recv_sem=out_recv.at[s],
+                    device_id={"chan": a},
+                    device_id_type=MESH,
+                ).start()
+
+    @pl.loop(0, seqs)
+    def _(s):
+        sent = gathered.at[s, pl.ds(0, na - blocks)]
+        pltpu.make_async_copy(sent, sent, fwd_send.at[s]).wait()
+        pltpu.make_async_copy(sent, sent, ret_send.at[s]).wait()
+        landed = out_ref.at[s, :, pl.ds(0, width * (n_chan - 1))]
+        pltpu.make_async_copy(landed, landed, out_send.at[s]).wait()
+        pltpu.make_async_copy(landed, landed, out_recv.at[s]).wait()
+        one = out_ref.at[s, :, pl.ds(0, width)]
+        pltpu.make_async_copy(one, one, out_local.at[s]).wait()
+
+    @pl.loop(0, units)
+    def _(k):
+        await_swap(k, perm1, c1_send)
+        await_swap(k, perm2, c2_send)
+
+
+def fused_layer(
+    inputs,
+    mix_first,
+    mix_second,
+    gate_scale,
+    gate_bias,
+    up_first,
+    up_second,
+    down_first,
+    down_second,
+):
+    n_seq, n_chan = lax.axis_size("seq"), lax.axis_size("chan")
+    seqs, rows, width = inputs.shape
+    blocks, group = mix_first.shape[0], mix_first.shape[1]
+    own_b, na = mix_second.shape[0], mix_second.shape[1]
+    parts = own_b // ROWS
+    units = seqs * blocks
+    by_row = jnp.swapaxes(mix_second.reshape(parts, ROWS, na, na), 1, 2)
+    bf = jnp.bfloat16
+    per_unit = pltpu.VMEM((units, group, width), bf)
+    per_b = pltpu.VMEM((seqs, na, own_b, width), bf)
+    dma = pltpu.SemaphoreType.DMA
+    return pl.pallas_call(
+        functools.partial(layer_kernel, n_seq, n_chan),
+        out_shape=jax.ShapeDtypeStruct((seqs, rows // n_chan, width * n_chan), bf),
+        in_specs=[pl.BlockSpec(memory_space=pltpu.VMEM)] * 9,
+        out_specs=pl.BlockSpec(memory_space=pl.ANY),
+        scratch_shapes=[
+            pltpu.VMEM((seqs, blocks, group, width), bf),
+            per_b,
+            per_b,
+            per_unit,
+            per_unit,
+            per_unit,
+            per_unit,
+            per_unit,
+            per_unit,
+            per_unit,
+            pltpu.VMEM(up_second.shape[1:], bf),
+            pltpu.VMEM(down_second.shape[1:], bf),
+            pltpu.VMEM((parts, na * ROWS, na * ROWS), bf),
+            pltpu.VMEM((group, width), jnp.float32),
+            dma((seqs,)),
+            dma((seqs,)),
+            dma((seqs,)),
+            dma((units,)),
+            dma((units,)),
+            dma((units,)),
+            dma((units,)),
+            dma((units,)),
+            dma((seqs,)),
+            dma((seqs,)),
+            dma((seqs,)),
+        ],
+        compiler_params=pltpu.CompilerParams(
+            collective_id=0, has_side_effects=True, vmem_limit_bytes=56 * 1024 * 1024
+        ),
+    )(
+        inputs.reshape(seqs, blocks, group, width),
+        mix_first,
+        by_row.reshape(parts, na * ROWS, na),
+        gate_scale.reshape(1, width),
+        gate_bias.reshape(1, width),
+        up_first[0],
+        up_second[0],
+        down_first[0],
+        down_second[0],
+    )
+
+
+def on_device(inputs, mix_first, mix_second, *rest):
+    fits = mix_second.shape[0] % ROWS == 0 and mix_first.shape[0] == lax.axis_size("chan")
+    run = fused_layer if fits else plain_layer
+    return run(inputs, mix_first, mix_second, *rest)
+
+
+def plain_layer(
     inputs,
     mix_first,
     mix_second,

time: 261 us -> 158 us (0.61); the launches traced: 256 us -> 157 us
  Pallas kernels: 0 us -> 152 us
  blocking collectives: 131 us -> 0 us
  waiting for transfers between devices: 41.5 us -> 0 us
  local copies, waits for them, and re-layouts: 43.4 us -> 4.91 us
  matrix products: 27.7 us -> 0 us
  starting transfers between devices: 10.9 us -> 0 us
    pallas_call x0 -> x1, Pallas kernels: none -> 152 us  [fused_layer(): pl.pallas_call(functools.partial(layer_kernel, n_seq, n_chan), out_shape=...]
    all_to_all x3 -> x0, blocking collectives: 131 us -> none  [the longest x1 51.5 us: on_device(): lax.all_to_all(first_pass, 'seq', split_axis=2, concat_axis=1, tiled=True)]
    all_to_all x2 -> x0, waiting for transfers between devices: 41.5 us -> none  [shard_monarch(): lax.all_to_all(inner_rows, 'chan', split_axis=2, concat_axis=2, tiled=True)]
    dot_general x5 -> x0, matrix products: 27.7 us -> none  [the longest x2 17.8 us: shard_monarch(): jnp.einsum('qp,stp->stq', inner_weight[0], values, preferred_element_type...]
    all_to_all x5 -> x0, local copies, waits for them, and re-layouts: 15 us -> none  [the longest x3 7.6 us: on_device(): lax.all_to_all(first_pass, 'seq', split_axis=2, concat_axis=1, tiled=True)]
    convert_element_type x4 -> x0, local copies, waits for them, and re-layouts: 11.2 us -> none  [the longest x1 6.21 us: on_device(): first_pass = jnp.einsum('abq,saqc->sabc', mix_first, grouped, preferred_e...]
    all_to_all x2 -> x0, starting transfers between devices: 10.9 us -> none  [shard_monarch(): lax.all_to_all(inner_rows, 'chan', split_axis=2, concat_axis=2, tiled=True)]
    reshape x2 -> x1, local copies, waits for them, and re-layouts: 7.9 us -> 1.76 us  [fused_layer(): by_row = jnp.swapaxes(mix_second.reshape(parts, ROWS, na, na), 1, 2)]
  transfers between devices with their start and end apart: 2 -> 0, of which waited for: 2 -> 0; matrix products, arithmetic and copies ran while one was open for 3% -> 0% of each run, Pallas kernels for 0% -> 0%
where the time goes in v1:
time: 158 us; the launch traced here: 157 us
  Pallas kernels  152 us (96%)
  local copies, waits for them, and re-layouts  4.91 us (3%)
    pallas_call x1, Pallas kernels, fused_layer(): pl.pallas_call(functools.partial(layer_kernel, n_seq, n_chan), out_shape=...  152 us

profile of v1, /device:TPU:29, one launch (start us, length us, event | category | flops | bytes accessed | tf_op | source)
XLA Modules:
  0.0 157.2 jit_solution(16136664687745050062)
XLA Ops:
  0.0 1.8 %copy.10 = bf16[2,16,32,32]{3,1,2,0:T(8,128)(2,1)} copy(bf16[2,16,32,32]{3,2,1,0:T(8,128)(2,1)} %bitcast.17) | data formatting | bytes 131072 | tf_op jit(solution)/shard_map/reshape | solution.py:287
  1.8 152.3 %shard_map.91 = bf16[2,256,2048]{2,1,0:T(8,128)(2,1)} custom-call(bf16[2,4,256,512]{3,2,1,0:T(8,128)(2,1)} %bitcast.11, bf16[4,256,256]{2,1,0:T(8,128)(2,1)} %mix1_ref.1, bf16[2,512,32]{2,1,0:T(8,128)(2,1)} %bitcast.14, f32[1,512]{1,0:T(1,128)} %bitcast.18, f32[1,512]{1,0:T(1,128)} %bitcast.19, bf16[512,512]{1,0:T(8,128)(2,1)} %bitcast.15, ...), custom_call_target="tpu_custom_call" | custom-call | tf_op jit(solution)/shard_map/pallas_call | solution.py:292
  154.1 3.2 %copy.12 = bf16[2,256,2048]{2,1,0:T(8,128)(2,1)} copy(bf16[2,256,2048]{2,1,0:T(8,128)(2,1)} %shard_map.91) | data formatting | bytes 4194304

commit v2 on v1

--- a/solution.py
+++ b/solution.py
@@ -9,6 +9,7 @@
 
 MESH = pl.DeviceIdType.MESH
 ROWS = 16
+AHEAD = 2
 
 
 def shard_monarch(values, inner_weight, outer_weight):
@@ -44,10 +45,10 @@
     mix2_ref,
     scale_ref,
     bias_ref,
-    up1_ref,
-    up2_ref,
-    down1_ref,
-    down2_ref,
+    up1_hbm,
+    up2_hbm,
+    down1_hbm,
+    down2_hbm,
     out_ref,
     first,
     gathered,
@@ -63,6 +64,11 @@
     down2p,
     spread,
     acc,
+    up1_ref,
+    up2_ref,
+    down1_ref,
+    down2_ref,
+    load_sem,
     fwd_send,
     fwd_recv,
     ret_send,
@@ -92,7 +98,15 @@
         pl.semaphore_signal(
             barrier, inc=1, device_id={"chan": lax.rem(me_c + i, n_chan)}, device_id_type=MESH
         )
-    pl.semaphore_wait(barrier, n_seq + n_chan - 2)
+
+    loads = [
+        pltpu.make_async_copy(src, dst, load_sem.at[i])
+        for i, (src, dst) in enumerate(
+            [(up2_hbm, up2_ref), (down2_hbm, down2_ref), (up1_hbm, up1_ref), (down1_hbm, down1_ref)]
+        )
+    ]
+    for load in loads:
+        load.start()
 
     my_b = pl.ds(pl.multiple_of(me_s * own_b, own_b), own_b)
     my_a = pl.ds(me_s * blocks, blocks)
@@ -104,26 +118,46 @@
         half = blocks // 2
         return lax.div(k, blocks), lax.rem(j, 2) * half + lax.div(j, 2)
 
-    @pl.loop(0, seqs)
-    def _(s):
+    parts = own_b // ROWS
+
+    def run_first(s):
         @pl.loop(0, blocks)
         def _(a):
             first[s, a] = dot(mix1_ref[a], x_ref[s, a]).astype(jnp.bfloat16)
 
+        gathered[s, my_a] = first[s, :, my_b, :]
+
+    def send_first(s, g):
+        landing = pl.ds(g * ROWS, ROWS)
+
         @pl.loop(1, n_seq)
         def _(i):
             other = lax.rem(me_s + i, n_seq)
-            rows = pl.ds(pl.multiple_of(other * own_b, own_b), own_b)
+            rows = pl.ds(pl.multiple_of(other * own_b + g * ROWS, ROWS), ROWS)
             pltpu.make_async_remote_copy(
                 src_ref=first.at[s, :, rows, :],
-                dst_ref=gathered.at[s, my_a],
-                send_sem=fwd_send.at[s],
-                recv_sem=fwd_recv.at[s],
+                dst_ref=gathered.at[s, my_a, landing, :],
+                send_sem=fwd_send.at[s * parts + g],
+                recv_sem=fwd_recv.at[s * parts + g],
                 device_id={"seq": other},
                 device_id_type=MESH,
             ).start()
 
-        gathered[s, my_a] = first[s, :, my_b, :]
+    def await_first(s, g, sem):
+        others = gathered.at[s, pl.ds(0, na - blocks), pl.ds(g * ROWS, ROWS), :]
+        pltpu.make_async_copy(others, others, sem.at[s * parts + g]).wait()
+
+    run_first(0)
+    pl.semaphore_wait(barrier, n_seq + n_chan - 2)
+    for g in range(parts):
+        send_first(0, g)
+
+    @pl.loop(1, seqs)
+    def _(s):
+        run_first(s)
+
+    for load in loads[:2]:
+        load.wait()
 
     span = na * ROWS
     row = lax.broadcasted_iota(jnp.int32, (width, width), 0)
@@ -143,38 +177,51 @@
     s_row = lax.broadcasted_iota(jnp.int32, (span, span), 0)
     s_col = lax.broadcasted_iota(jnp.int32, (span, span), 1)
 
-    @pl.loop(0, own_b // ROWS)
+    @pl.loop(0, parts)
     def _(g):
         wide = dot(mix2_ref[g], expand)
         spread[g] = jnp.where(s_row % ROWS == s_col % ROWS, wide, 0.0).astype(jnp.bfloat16)
 
-    @pl.loop(0, seqs)
-    def _(s):
-        others = gathered.at[s, pl.ds(0, na - blocks)]
-        pltpu.make_async_copy(others, others, fwd_recv.at[s]).wait()
-        for g in range(own_b // ROWS):
-            part = gathered[s, :, g * ROWS : (g + 1) * ROWS, :].reshape(span, width)
+    for load in loads[2:]:
+        load.wait()
+
+    def run_second(s):
+        for g in range(parts):
+            rows = slice(g * ROWS, (g + 1) * ROWS)
+            await_first(s, g, fwd_recv)
+            if g == 0:
+
+                @pl.when(s + 1 < seqs)
+                def _():
+                    send_first(s + 1, 0)
+
+            part = gathered[s, :, rows, :].reshape(span, width)
             got = dot(spread[g], part).astype(jnp.bfloat16)
-            second[s, :, g * ROWS : (g + 1) * ROWS, :] = got.reshape(na, ROWS, width)
-
-        @pl.loop(0, blocks)
-        def _(j):
-            k = s * blocks + j
+            second[s, :, rows, :] = got.reshape(na, ROWS, width)
+
+        @pl.loop(s * blocks, (s + 1) * blocks)
+        def _(k):
             _, a = unit_of(k)
-
-            @pl.loop(1, n_seq)
-            def _(i):
-                other = lax.rem(me_s + i, n_seq)
-                pltpu.make_async_remote_copy(
-                    src_ref=second.at[s, other * blocks + a],
-                    dst_ref=mixed.at[k, my_b, :],
-                    send_sem=ret_send.at[s],
-                    recv_sem=ret_recv.at[k],
-                    device_id={"seq": other},
-                    device_id_type=MESH,
-                ).start()
-
             mixed[k, my_b, :] = second[s, me_s * blocks + a]
+
+    def send_second(k):
+        s, a = unit_of(k)
+
+        @pl.loop(1, n_seq)
+        def _(i):
+            other = lax.rem(me_s + i, n_seq)
+            pltpu.make_async_remote_copy(
+                src_ref=second.at[s, other * blocks + a],
+                dst_ref=mixed.at[k, my_b, :],
+                send_sem=ret_send.at[k],
+                recv_sem=ret_recv.at[k],
+                device_id={"seq": other},
+                device_id_type=MESH,
+            ).start()
+
+    def await_second(k, sem):
+        others = mixed.at[k, pl.ds(0, group - own_b), :]
+        pltpu.make_async_copy(others, others, sem.at[k]).wait()
 
     def swap(k, src, dst, send_sem, recv_sem):
         @pl.loop(1, n_chan)
@@ -202,8 +249,26 @@
         def _():
             k = step
             s, a = unit_of(k)
-            others = mixed.at[k, pl.ds(0, group - own_b), :]
-            pltpu.make_async_copy(others, others, ret_recv.at[k]).wait()
+            j = lax.rem(k, blocks)
+
+            @pl.when(j == 0)
+            def _():
+                run_second(s)
+
+                @pl.loop(0, AHEAD)
+                def _(i):
+                    send_second(k + i)
+
+            @pl.when(j + AHEAD < blocks)
+            def _():
+                send_second(k + AHEAD)
+
+            @pl.when((j == 1) & (s + 1 < seqs))
+            def _():
+                for g in range(1, parts):
+                    send_first(s + 1, g)
+
+            await_second(k, ret_recv)
             x = x_ref[s, a].astype(jnp.float32)
             gate = jax.nn.sigmoid(scale_ref[...] * x + bias_ref[...])
             hidden[k] = (x + mixed[k].astype(jnp.float32) * gate).astype(jnp.bfloat16)
@@ -252,9 +317,8 @@
 
     @pl.loop(0, seqs)
     def _(s):
-        sent = gathered.at[s, pl.ds(0, na - blocks)]
-        pltpu.make_async_copy(sent, sent, fwd_send.at[s]).wait()
-        pltpu.make_async_copy(sent, sent, ret_send.at[s]).wait()
+        for g in range(parts):
+            await_first(s, g, fwd_send)
         landed = out_ref.at[s, :, pl.ds(0, width * (n_chan - 1))]
         pltpu.make_async_copy(landed, landed, out_send.at[s]).wait()
         pltpu.make_async_copy(landed, landed, out_recv.at[s]).wait()
@@ -263,6 +327,7 @@
 
     @pl.loop(0, units)
     def _(k):
+        await_second(k, ret_send)
         await_swap(k, perm1, c1_send)
         await_swap(k, perm2, c2_send)
 
@@ -292,7 +357,8 @@
     return pl.pallas_call(
         functools.partial(layer_kernel, n_seq, n_chan),
         out_shape=jax.ShapeDtypeStruct((seqs, rows // n_chan, width * n_chan), bf),
-        in_specs=[pl.BlockSpec(memory_space=pltpu.VMEM)] * 9,
+        in_specs=[pl.BlockSpec(memory_space=pltpu.VMEM)] * 5
+        + [pl.BlockSpec(memory_space=pl.ANY)] * 4,
         out_specs=pl.BlockSpec(memory_space=pl.ANY),
         scratch_shapes=[
             pltpu.VMEM((seqs, blocks, group, width), bf),
@@ -309,9 +375,14 @@
             pltpu.VMEM(down_second.shape[1:], bf),
             pltpu.VMEM((parts, na * ROWS, na * ROWS), bf),
             pltpu.VMEM((group, width), jnp.float32),
-            dma((seqs,)),
-            dma((seqs,)),
-            dma((seqs,)),
+            pltpu.VMEM(up_first.shape[1:], bf),
+            pltpu.VMEM(up_second.shape[1:], bf),
+            pltpu.VMEM(down_first.shape[1:], bf),
+            pltpu.VMEM(down_second.shape[1:], bf),
+            dma((4,)),
+            dma((seqs * parts,)),
+            dma((seqs * parts,)),
+            dma((units,)),
             dma((units,)),
             dma((units,)),
             dma((units,)),

time: 158 us -> 138 us (0.87)
  Pallas kernels: 152 us -> 132 us
    pallas_call x1, Pallas kernels: 152 us -> 132 us  [fused_layer(): pl.pallas_call(functools.partial(layer_kernel, n_seq, n_chan), out_shape=...]
where the time goes in v2:
time: 138 us; the launch traced here: 137 us
  Pallas kernels  132 us (96%)
  local copies, waits for them, and re-layouts  4.91 us (4%)
    pallas_call x1, Pallas kernels, fused_layer(): pl.pallas_call(functools.partial(layer_kernel, n_seq, n_chan), out_shape=...  132 us
    unnamed x1, local copies, waits for them, and re-layouts  3.16 us

profile of v2, /device:TPU:29, one launch (start us, length us, event | category | flops | bytes accessed | tf_op | source)
XLA Modules:
  0.0 136.7 jit_solution(13893000701326333925)
XLA Ops:
  0.0 1.8 %copy.10 = bf16[2,16,32,32]{3,1,2,0:T(8,128)(2,1)} copy(bf16[2,16,32,32]{3,2,1,0:T(8,128)(2,1)} %bitcast.17) | data formatting | bytes 131072 | tf_op jit(solution)/shard_map/reshape | solution.py:352
  1.8 131.8 %shard_map.91 = bf16[2,256,2048]{2,1,0:T(8,128)(2,1)} custom-call(bf16[2,4,256,512]{3,2,1,0:T(8,128)(2,1)} %bitcast.11, bf16[4,256,256]{2,1,0:T(8,128)(2,1)} %mix1_ref.1, bf16[2,512,32]{2,1,0:T(8,128)(2,1)} %bitcast.14, f32[1,512]{1,0:T(1,128)} %bitcast.18, f32[1,512]{1,0:T(1,128)} %bitcast.19, bf16[512,512]{1,0:T(8,128)(2,1)} %bitcast.15, ...), custom_call_target="tpu_custom_call" | custom-call | tf_op jit(solution)/shard_map/pallas_call | solution.py:357
  133.6 3.2 %copy.12 = bf16[2,256,2048]{2,1,0:T(8,128)(2,1)} copy(bf16[2,256,2048]{2,1,0:T(8,128)(2,1)} %shard_map.91) | data formatting | bytes 4194304

commit v3 on v2

--- a/solution.py
+++ b/solution.py
@@ -9,6 +9,7 @@
 
 MESH = pl.DeviceIdType.MESH
 ROWS = 16
+LANES = 2
 AHEAD = 2
 
 
@@ -81,11 +82,14 @@
     out_recv,
     out_local,
 ):
-    seqs, blocks, group, width = x_ref.shape
+    seqs, blocks, _, parts, _, width = x_ref.shape
     na = n_seq * blocks
-    own_b = group // n_seq
+    group = n_seq * parts * ROWS
     sub = width // n_chan
-    units = seqs * blocks
+    chunks = seqs * parts
+    units = chunks * LANES
+    paired = blocks // LANES
+    half = n_seq * ROWS
     me_s = lax.axis_index("seq")
     me_c = lax.axis_index("chan")
 
@@ -108,49 +112,40 @@
     for load in loads:
         load.start()
 
-    my_b = pl.ds(pl.multiple_of(me_s * own_b, own_b), own_b)
     my_a = pl.ds(me_s * blocks, blocks)
     my_sub = pl.ds(pl.multiple_of(me_c * sub, sub), sub)
     my_cols = pl.ds(pl.multiple_of(me_c * width, width), width)
 
-    def unit_of(k):
-        j = lax.rem(k, blocks)
-        half = blocks // 2
-        return lax.div(k, blocks), lax.rem(j, 2) * half + lax.div(j, 2)
-
-    parts = own_b // ROWS
-
     def run_first(s):
         @pl.loop(0, blocks)
         def _(a):
-            first[s, a] = dot(mix1_ref[a], x_ref[s, a]).astype(jnp.bfloat16)
-
-        gathered[s, my_a] = first[s, :, my_b, :]
-
-    def send_first(s, g):
-        landing = pl.ds(g * ROWS, ROWS)
-
+            got = dot(mix1_ref[a], x_ref[s, a].reshape(group, width)).astype(jnp.bfloat16)
+            first[s, a] = got.reshape(n_seq, parts, ROWS, width)
+
+        for g in range(parts):
+            gathered[s * parts + g, my_a] = first[s, :, me_s, g]
+
+    def send_first(q):
         @pl.loop(1, n_seq)
         def _(i):
             other = lax.rem(me_s + i, n_seq)
-            rows = pl.ds(pl.multiple_of(other * own_b + g * ROWS, ROWS), ROWS)
             pltpu.make_async_remote_copy(
-                src_ref=first.at[s, :, rows, :],
-                dst_ref=gathered.at[s, my_a, landing, :],
-                send_sem=fwd_send.at[s * parts + g],
-                recv_sem=fwd_recv.at[s * parts + g],
+                src_ref=first.at[lax.div(q, parts), :, other, lax.rem(q, parts)],
+                dst_ref=gathered.at[q, my_a],
+                send_sem=fwd_send.at[q],
+                recv_sem=fwd_recv.at[q],
                 device_id={"seq": other},
                 device_id_type=MESH,
             ).start()
 
-    def await_first(s, g, sem):
-        others = gathered.at[s, pl.ds(0, na - blocks), pl.ds(g * ROWS, ROWS), :]
-        pltpu.make_async_copy(others, others, sem.at[s * parts + g]).wait()
+    def await_first(q, sem):
+        others = gathered.at[q, pl.ds(0, na - blocks)]
+        pltpu.make_async_copy(others, others, sem.at[q]).wait()
 
     run_first(0)
     pl.semaphore_wait(barrier, n_seq + n_chan - 2)
-    for g in range(parts):
-        send_first(0, g)
+    for q in range(min(AHEAD, parts)):
+        send_first(jnp.int32(q))
 
     @pl.loop(1, seqs)
     def _(s):
@@ -185,34 +180,27 @@
     for load in loads[2:]:
         load.wait()
 
-    def run_second(s):
-        for g in range(parts):
-            rows = slice(g * ROWS, (g + 1) * ROWS)
-            await_first(s, g, fwd_recv)
-            if g == 0:
-
-                @pl.when(s + 1 < seqs)
-                def _():
-                    send_first(s + 1, 0)
-
-            part = gathered[s, :, rows, :].reshape(span, width)
-            got = dot(spread[g], part).astype(jnp.bfloat16)
-            second[s, :, rows, :] = got.reshape(na, ROWS, width)
-
-        @pl.loop(s * blocks, (s + 1) * blocks)
-        def _(k):
-            _, a = unit_of(k)
-            mixed[k, my_b, :] = second[s, me_s * blocks + a]
-
-    def send_second(k):
-        s, a = unit_of(k)
+    def run_second(q):
+        await_first(q, fwd_recv)
+        part = gathered[q].reshape(span, width)
+        got = dot(spread[lax.rem(q, parts)], part).astype(jnp.bfloat16)
+        second[q] = got.reshape(n_seq, paired, LANES, ROWS, width)
+
+        @pl.loop(0, LANES)
+        def _(lane):
+            k = q * LANES + lane
+            mixed[k, :, me_s] = second[q, me_s, :, lane]
+            send_second(q, lane)
+
+    def send_second(q, lane):
+        k = q * LANES + lane
 
         @pl.loop(1, n_seq)
         def _(i):
             other = lax.rem(me_s + i, n_seq)
             pltpu.make_async_remote_copy(
-                src_ref=second.at[s, other * blocks + a],
-                dst_ref=mixed.at[k, my_b, :],
+                src_ref=second.at[q, other, :, lane],
+                dst_ref=mixed.at[k, :, me_s],
                 send_sem=ret_send.at[k],
                 recv_sem=ret_recv.at[k],
                 device_id={"seq": other},
@@ -220,7 +208,7 @@
             ).start()
 
     def await_second(k, sem):
-        others = mixed.at[k, pl.ds(0, group - own_b), :]
+        others = mixed.at[k, :, pl.ds(0, n_seq - 1)]
         pltpu.make_async_copy(others, others, sem.at[k]).wait()
 
     def swap(k, src, dst, send_sem, recv_sem):
@@ -248,30 +236,23 @@
         @pl.when(step < units)
         def _():
             k = step
-            s, a = unit_of(k)
-            j = lax.rem(k, blocks)
-
-            @pl.when(j == 0)
+            q, lane = lax.div(k, LANES), lax.rem(k, LANES)
+            s, g = lax.div(q, parts), lax.rem(q, parts)
+
+            @pl.when(lane == 0)
             def _():
-                run_second(s)
-
-                @pl.loop(0, AHEAD)
-                def _(i):
-                    send_second(k + i)
-
-            @pl.when(j + AHEAD < blocks)
+                run_second(q)
+
+            @pl.when((lane == 1) & (q + AHEAD < chunks))
             def _():
-                send_second(k + AHEAD)
-
-            @pl.when((j == 1) & (s + 1 < seqs))
-            def _():
-                for g in range(1, parts):
-                    send_first(s + 1, g)
+                send_first(q + AHEAD)
 
             await_second(k, ret_recv)
-            x = x_ref[s, a].astype(jnp.float32)
-            gate = jax.nn.sigmoid(scale_ref[...] * x + bias_ref[...])
-            hidden[k] = (x + mixed[k].astype(jnp.float32) * gate).astype(jnp.bfloat16)
+            for pair in range(paired):
+                x = x_ref[s, pair * LANES + lane, :, g].reshape(half, width).astype(jnp.float32)
+                gate = jax.nn.sigmoid(scale_ref[...] * x + bias_ref[...])
+                mix = mixed[k, pair].reshape(half, width).astype(jnp.float32)
+                hidden[k, pair * half : (pair + 1) * half] = (x + mix * gate).astype(jnp.bfloat16)
             inner1[k] = dot_t(hidden[k], up1_ref[...]).astype(jnp.bfloat16)
             swap(k, inner1, perm1, c1_send, c1_recv)
 
@@ -293,37 +274,42 @@
         @pl.when(step >= 2)
         def _():
             k = step - 2
-            s, a = unit_of(k)
+            q, lane = lax.div(k, LANES), lax.rem(k, LANES)
+            s, g = lax.div(q, parts), lax.rem(q, parts)
             await_swap(k, perm2, c2_recv)
             got = dot_t(perm2[k], down2p[...])
-            result[k] = (hidden[k].astype(jnp.float32) + got).astype(jnp.bfloat16)
-
-            @pl.when(a == me_c)
-            def _():
-                pltpu.make_async_copy(
-                    result.at[k], out_ref.at[s, :, my_cols], out_local.at[s]
-                ).start()
-
-            @pl.when(a != me_c)
-            def _():
-                pltpu.make_async_remote_copy(
-                    src_ref=result.at[k],
-                    dst_ref=out_ref.at[s, :, my_cols],
-                    send_sem=out_send.at[s],
-                    recv_sem=out_recv.at[s],
-                    device_id={"chan": a},
-                    device_id_type=MESH,
-                ).start()
+            got = (hidden[k].astype(jnp.float32) + got).astype(jnp.bfloat16)
+            result[k] = got.reshape(paired, n_seq, ROWS, width)
+            for pair in range(paired):
+                a = pair * LANES + lane
+                src, dst = result.at[k, pair], out_ref.at[s, :, g, :, my_cols]
+
+                @pl.when(a == me_c)
+                def _(src=src, dst=dst):
+                    pltpu.make_async_copy(src, dst, out_local.at[s]).start()
+
+                @pl.when(a != me_c)
+                def _(src=src, dst=dst, a=a):
+                    pltpu.make_async_remote_copy(
+                        src_ref=src,
+                        dst_ref=dst,
+                        send_sem=out_send.at[s],
+                        recv_sem=out_recv.at[s],
+                        device_id={"chan": a},
+                        device_id_type=MESH,
+                    ).start()
 
     @pl.loop(0, seqs)
     def _(s):
-        for g in range(parts):
-            await_first(s, g, fwd_send)
-        landed = out_ref.at[s, :, pl.ds(0, width * (n_chan - 1))]
+        landed = out_ref.at[s, :, :, :, pl.ds(0, width * (n_chan - 1))]
         pltpu.make_async_copy(landed, landed, out_send.at[s]).wait()
         pltpu.make_async_copy(landed, landed, out_recv.at[s]).wait()
-        one = out_ref.at[s, :, pl.ds(0, width)]
+        one = out_ref.at[s, :, :, :, pl.ds(0, width)]
         pltpu.make_async_copy(one, one, out_local.at[s]).wait()
+
+    @pl.loop(0, chunks)
+    def _(q):
+        await_first(q, fwd_send)
 
     @pl.loop(0, units)
     def _(k):
@@ -348,40 +334,42 @@
     blocks, group = mix_first.shape[0], mix_first.shape[1]
     own_b, na = mix_second.shape[0], mix_second.shape[1]
     parts = own_b // ROWS
-    units = seqs * blocks
+    chunks = seqs * parts
+    units = chunks * LANES
+    paired = blocks // LANES
     by_row = jnp.swapaxes(mix_second.reshape(parts, ROWS, na, na), 1, 2)
     bf = jnp.bfloat16
-    per_unit = pltpu.VMEM((units, group, width), bf)
-    per_b = pltpu.VMEM((seqs, na, own_b, width), bf)
+    per_unit = pltpu.VMEM((units, paired * n_seq * ROWS, width), bf)
+    by_device = pltpu.VMEM((units, paired, n_seq, ROWS, width), bf)
     dma = pltpu.SemaphoreType.DMA
-    return pl.pallas_call(
+    out = pl.pallas_call(
         functools.partial(layer_kernel, n_seq, n_chan),
-        out_shape=jax.ShapeDtypeStruct((seqs, rows // n_chan, width * n_chan), bf),
+        out_shape=jax.ShapeDtypeStruct((seqs, n_seq, parts, ROWS, width * n_chan), bf),
         in_specs=[pl.BlockSpec(memory_space=pltpu.VMEM)] * 5
         + [pl.BlockSpec(memory_space=pl.ANY)] * 4,
         out_specs=pl.BlockSpec(memory_space=pl.ANY),
         scratch_shapes=[
-            pltpu.VMEM((seqs, blocks, group, width), bf),
-            per_b,
-            per_b,
+            pltpu.VMEM((seqs, blocks, n_seq, parts, ROWS, width), bf),
+            pltpu.VMEM((chunks, na, ROWS, width), bf),
+            pltpu.VMEM((chunks, n_seq, paired, LANES, ROWS, width), bf),
+            by_device,
             per_unit,
             per_unit,
             per_unit,
             per_unit,
             per_unit,
-            per_unit,
-            per_unit,
+            by_device,
             pltpu.VMEM(up_second.shape[1:], bf),
             pltpu.VMEM(down_second.shape[1:], bf),
             pltpu.VMEM((parts, na * ROWS, na * ROWS), bf),
-            pltpu.VMEM((group, width), jnp.float32),
+            pltpu.VMEM((paired * n_seq * ROWS, width), jnp.float32),
             pltpu.VMEM(up_first.shape[1:], bf),
             pltpu.VMEM(up_second.shape[1:], bf),
             pltpu.VMEM(down_first.shape[1:], bf),
             pltpu.VMEM(down_second.shape[1:], bf),
             dma((4,)),
-            dma((seqs * parts,)),
-            dma((seqs * parts,)),
+            dma((chunks,)),
+            dma((chunks,)),
             dma((units,)),
             dma((units,)),
             dma((units,)),
@@ -396,7 +384,7 @@
             collective_id=0, has_side_effects=True, vmem_limit_bytes=56 * 1024 * 1024
         ),
     )(
-        inputs.reshape(seqs, blocks, group, width),
+        inputs.reshape(seqs, blocks, n_seq, parts, ROWS, width),
         mix_first,
         by_row.reshape(parts, na * ROWS, na),
         gate_scale.reshape(1, width),
@@ -406,10 +394,13 @@
         down_first[0],
         down_second[0],
     )
+    return out.reshape(seqs, group, width * n_chan)
 
 
 def on_device(inputs, mix_first, mix_second, *rest):
-    fits = mix_second.shape[0] % ROWS == 0 and mix_first.shape[0] == lax.axis_size("chan")
+    blocks = mix_first.shape[0]
+    whole = mix_second.shape[0] % ROWS == 0 and blocks % LANES == 0
+    fits = whole and blocks == lax.axis_size("chan")
     run = fused_layer if fits else plain_layer
     return run(inputs, mix_first, mix_second, *rest)
 

time: 138 us -> 136 us (0.986)
  no operation moved by 1% of the time
where the time goes in v3:
time: 136 us
  Pallas kernels  131 us (96%)
  local copies, waits for them, and re-layouts  4.91 us (4%)
    pallas_call x1, Pallas kernels, fused_layer(): pl.pallas_call(functools.partial(layer_kernel, n_seq, n_chan), out_shape=...  131 us
    unnamed x1, local copies, waits for them, and re-layouts  3.16 us

profile of v3, /device:TPU:29, one launch (start us, length us, event | category | flops | bytes accessed | tf_op | source)
XLA Modules:
  0.0 135.8 jit_solution(5771689836407430978)
XLA Ops:
  0.0 1.8 %copy.10 = bf16[2,16,32,32]{3,1,2,0:T(8,128)(2,1)} copy(bf16[2,16,32,32]{3,2,1,0:T(8,128)(2,1)} %bitcast.19) | data formatting | bytes 131072 | tf_op jit(solution)/shard_map/reshape | solution.py:340
  1.8 130.9 %shard_map.91 = bf16[2,8,2,16,2048]{4,3,2,1,0:T(8,128)(2,1)} custom-call(bf16[2,4,8,2,16,512]{5,4,3,2,1,0:T(8,128)(2,1)} %bitcast.13, bf16[4,256,256]{2,1,0:T(8,128)(2,1)} %mix1_ref.1, bf16[2,512,32]{2,1,0:T(8,128)(2,1)} %bitcast.16, f32[1,512]{1,0:T(1,128)} %bitcast.20, f32[1,512]{1,0:T(1,128)} %bitcast.21, bf16[512,512]{1,0:T(8,128)(2,1)} %bitcast.17, ...), custom_call_target="tpu_custom_call" | custom-call | tf_op jit(solution)/shard_map/pallas_call | solution.py:345
  132.7 3.2 %copy.12 = bf16[2,256,2048]{2,1,0:T(8,128)(2,1)} copy(bf16[2,256,2048]{2,1,0:T(8,128)(2,1)} %bitcast.12) | data formatting | bytes 4194304

commit v4 on v3

--- a/solution.py
+++ b/solution.py
@@ -172,9 +172,12 @@
     s_row = lax.broadcasted_iota(jnp.int32, (span, span), 0)
     s_col = lax.broadcasted_iota(jnp.int32, (span, span), 1)
 
+    turn = (s_col == (s_row % ROWS) * na + s_row // ROWS).astype(jnp.float32).astype(jnp.bfloat16)
+
     @pl.loop(0, parts)
     def _(g):
-        wide = dot(mix2_ref[g], expand)
+        by_row = dot(turn, mix2_ref[g]).astype(jnp.bfloat16)
+        wide = dot(by_row, expand)
         spread[g] = jnp.where(s_row % ROWS == s_col % ROWS, wide, 0.0).astype(jnp.bfloat16)
 
     for load in loads[2:]:
@@ -231,6 +234,8 @@
         others = dst.at[k, :, pl.ds(0, width - sub)]
         pltpu.make_async_copy(others, others, sem.at[k]).wait()
 
+    run_second(jnp.int32(0))
+
     @pl.loop(0, units + 2)
     def _(step):
         @pl.when(step < units)
@@ -239,13 +244,13 @@
             q, lane = lax.div(k, LANES), lax.rem(k, LANES)
             s, g = lax.div(q, parts), lax.rem(q, parts)
 
-            @pl.when(lane == 0)
-            def _():
-                run_second(q)
-
             @pl.when((lane == 1) & (q + AHEAD < chunks))
             def _():
                 send_first(q + AHEAD)
+
+            @pl.when((lane == 1) & (q + 1 < chunks))
+            def _():
+                run_second(q + 1)
 
             await_second(k, ret_recv)
             for pair in range(paired):
@@ -337,7 +342,6 @@
     chunks = seqs * parts
     units = chunks * LANES
     paired = blocks // LANES
-    by_row = jnp.swapaxes(mix_second.reshape(parts, ROWS, na, na), 1, 2)
     bf = jnp.bfloat16
     per_unit = pltpu.VMEM((units, paired * n_seq * ROWS, width), bf)
     by_device = pltpu.VMEM((units, paired, n_seq, ROWS, width), bf)
@@ -386,7 +390,7 @@
     )(
         inputs.reshape(seqs, blocks, n_seq, parts, ROWS, width),
         mix_first,
-        by_row.reshape(parts, na * ROWS, na),
+        mix_second.reshape(parts, ROWS * na, na),
         gate_scale.reshape(1, width),
         gate_bias.reshape(1, width),
         up_first[0],

time: 136 us -> 136 us (level)
  local copies, waits for them, and re-layouts: 4.91 us -> 3.16 us
    reshape x1 -> x0, local copies, waits for them, and re-layouts: 1.76 us -> none  [fused_layer(): by_row = jnp.swapaxes(mix_second.reshape(parts, ROWS, na, na), 1, 2)]
    pallas_call x1, Pallas kernels: 131 us -> 132 us  [fused_layer(): pl.pallas_call(functools.partial(layer_kernel, n_seq, n_chan), out_shape=...]
where the time goes in v4:
time: 136 us
  Pallas kernels  132 us (97%)
  local copies, waits for them, and re-layouts  3.16 us (2%)
    pallas_call x1, Pallas kernels, fused_layer(): pl.pallas_call(functools.partial(layer_kernel, n_seq, n_chan), out_shape=...  132 us
    unnamed x1, local copies, waits for them, and re-layouts  3.16 us

profile of v4, /device:TPU:29, one launch (start us, length us, event | category | flops | bytes accessed | tf_op | source)
XLA Modules:
  0.0 135.6 jit_solution(5889141667326780978)
XLA Ops:
  0.0 132.4 %shard_map.91 = bf16[2,8,2,16,2048]{4,3,2,1,0:T(8,128)(2,1)} custom-call(bf16[2,4,8,2,16,512]{5,4,3,2,1,0:T(8,128)(2,1)} %bitcast.10, bf16[4,256,256]{2,1,0:T(8,128)(2,1)} %mix1_ref.1, bf16[2,512,32]{2,1,0:T(8,128)(2,1)} %bitcast.15, f32[1,512]{1,0:T(1,128)} %bitcast.16, f32[1,512]{1,0:T(1,128)} %bitcast.17, bf16[512,512]{1,0:T(8,128)(2,1)} %bitcast.13, ...), custom_call_target="tpu_custom_call" | custom-call | tf_op jit(solution)/shard_map/pallas_call | solution.py:349
  132.4 3.2 %copy.11 = bf16[2,256,2048]{2,1,0:T(8,128)(2,1)} copy(bf16[2,256,2048]{2,1,0:T(8,128)(2,1)} %bitcast.9) | data formatting | bytes 4194304

commit v5 on v4

--- a/solution.py
+++ b/solution.py
@@ -11,6 +11,7 @@
 ROWS = 16
 LANES = 2
 AHEAD = 2
+STRIDE = 3
 
 
 def shard_monarch(values, inner_weight, outer_weight):
@@ -128,7 +129,7 @@
     def send_first(q):
         @pl.loop(1, n_seq)
         def _(i):
-            other = lax.rem(me_s + i, n_seq)
+            other = lax.rem(me_s + STRIDE * i, n_seq)
             pltpu.make_async_remote_copy(
                 src_ref=first.at[lax.div(q, parts), :, other, lax.rem(q, parts)],
                 dst_ref=gathered.at[q, my_a],
@@ -200,7 +201,7 @@
 
         @pl.loop(1, n_seq)
         def _(i):
-            other = lax.rem(me_s + i, n_seq)
+            other = lax.rem(me_s + STRIDE * i, n_seq)
             pltpu.make_async_remote_copy(
                 src_ref=second.at[q, other, :, lane],
                 dst_ref=mixed.at[k, :, me_s],
@@ -404,7 +405,7 @@
 def on_device(inputs, mix_first, mix_second, *rest):
     blocks = mix_first.shape[0]
     whole = mix_second.shape[0] % ROWS == 0 and blocks % LANES == 0
-    fits = whole and blocks == lax.axis_size("chan")
+    fits = whole and blocks == lax.axis_size("chan") and lax.axis_size("seq") % STRIDE != 0
     run = fused_layer if fits else plain_layer
     return run(inputs, mix_first, mix_second, *rest)
 

time: 136 us -> 132 us (0.971)
  Pallas kernels: 132 us -> 128 us
    pallas_call x1, Pallas kernels: 132 us -> 128 us  [fused_layer(): pl.pallas_call(functools.partial(layer_kernel, n_seq, n_chan), out_shape=...]
where the time goes in v5:
time: 132 us; the launch traced here: 131 us
  Pallas kernels  128 us (97%)
  local copies, waits for them, and re-layouts  3.16 us (2%)
    pallas_call x1, Pallas kernels, fused_layer(): pl.pallas_call(functools.partial(layer_kernel, n_seq, n_chan), out_shape=...  128 us
    unnamed x1, local copies, waits for them, and re-layouts  3.16 us

profile of v5, /device:TPU:29, one launch (start us, length us, event | category | flops | bytes accessed | tf_op | source)
XLA Modules:
  0.0 131.4 jit_solution(12090189699382702530)
XLA Ops:
  0.0 128.3 %shard_map.91 = bf16[2,8,2,16,2048]{4,3,2,1,0:T(8,128)(2,1)} custom-call(bf16[2,4,8,2,16,512]{5,4,3,2,1,0:T(8,128)(2,1)} %bitcast.10, bf16[4,256,256]{2,1,0:T(8,128)(2,1)} %mix1_ref.1, bf16[2,512,32]{2,1,0:T(8,128)(2,1)} %bitcast.15, f32[1,512]{1,0:T(1,128)} %bitcast.16, f32[1,512]{1,0:T(1,128)} %bitcast.17, bf16[512,512]{1,0:T(8,128)(2,1)} %bitcast.13, ...), custom_call_target="tpu_custom_call" | custom-call | tf_op jit(solution)/shard_map/pallas_call | solution.py:350
  128.3 3.2 %copy.11 = bf16[2,256,2048]{2,1,0:T(8,128)(2,1)} copy(bf16[2,256,2048]{2,1,0:T(8,128)(2,1)} %bitcast.9) | data formatting | bytes 4194304

commit v6 on v5

--- a/solution.py
+++ b/solution.py
@@ -268,7 +268,7 @@
             await_swap(k, perm1, c1_recv)
             acc[...] = jnp.zeros_like(acc)
 
-            @pl.loop(0, up2_ref.shape[0] // width)
+            @pl.loop(0, up2_ref.shape[0] // width, unroll=True)
             def _(t):
                 tile = pl.ds(pl.multiple_of(t * width, width), width)
                 act = jax.nn.gelu(dot_t(perm1[k], up2p[tile, :]), approximate=True)
@@ -322,6 +322,22 @@
         await_second(k, ret_send)
         await_swap(k, perm1, c1_send)
         await_swap(k, perm2, c2_send)
+
+
+def copy_kernel(src_ref, dst_ref):
+    dst_ref[...] = src_ref[...]
+
+
+def hand_over(array):
+    seqs, rows, width = array.shape
+    block = pl.BlockSpec((1, rows // 2, width), lambda s, i: (s, i, 0))
+    return pl.pallas_call(
+        copy_kernel,
+        out_shape=jax.ShapeDtypeStruct(array.shape, array.dtype),
+        grid=(seqs, 2),
+        in_specs=[block],
+        out_specs=block,
+    )(array)
 
 
 def fused_layer(
@@ -399,7 +415,7 @@
         down_first[0],
         down_second[0],
     )
-    return out.reshape(seqs, group, width * n_chan)
+    return hand_over(out.reshape(seqs, group, width * n_chan))
 
 
 def on_device(inputs, mix_first, mix_second, *rest):

time: 132 us -> 132 us (level)
  local copies, waits for them, and re-layouts: 3.16 us -> 0 us
  Pallas kernels: 128 us -> 131 us
    pallas_call x0 -> x1, Pallas kernels: none -> 3.79 us  [hand_over(): pl.pallas_call(copy_kernel, out_shape=jax.ShapeDtypeStruct(array.shape, a...]
    unnamed x1 -> x0, local copies, waits for them, and re-layouts: 3.16 us -> none
where the time goes in v6:
time: 132 us; the launch traced here: 131 us
  Pallas kernels  131 us (99%)
    pallas_call x1, Pallas kernels, fused_layer(): pl.pallas_call(functools.partial(layer_kernel, n_seq, n_chan), out_shape=...  127 us
    pallas_call x1, Pallas kernels, hand_over(): pl.pallas_call(copy_kernel, out_shape=jax.ShapeDtypeStruct(array.shape, a...  3.79 us

profile of v6, /device:TPU:29, one launch (start us, length us, event | category | flops | bytes accessed | tf_op | source)
XLA Modules:
  0.0 131.2 jit_solution(11448914017999655457)
XLA Ops:
  0.0 127.4 %shard_map.91 = bf16[2,8,2,16,2048]{4,3,2,1,0:T(8,128)(2,1)} custom-call(bf16[2,4,8,2,16,512]{5,4,3,2,1,0:T(8,128)(2,1)} %bitcast.10, bf16[4,256,256]{2,1,0:T(8,128)(2,1)} %mix1_ref.1, bf16[2,512,32]{2,1,0:T(8,128)(2,1)} %bitcast.15, f32[1,512]{1,0:T(1,128)} %bitcast.16, f32[1,512]{1,0:T(1,128)} %bitcast.17, bf16[512,512]{1,0:T(8,128)(2,1)} %bitcast.13, ...), custom_call_target="tpu_custom_call" | custom-call | tf_op jit(solution)/shard_map/pallas_call | solution.py:366
  127.4 3.8 %shard_map.92 = bf16[2,256,2048]{2,1,0:T(8,128)(2,1)} custom-call(bf16[2,256,2048]{2,1,0:T(8,128)(2,1)} %bitcast.9), custom_call_target="tpu_custom_call" | custom-call | tf_op jit(solution)/shard_map/pallas_call | solution.py:334

commit v7 on v5

--- a/solution.py
+++ b/solution.py
@@ -268,7 +268,7 @@
             await_swap(k, perm1, c1_recv)
             acc[...] = jnp.zeros_like(acc)
 
-            @pl.loop(0, up2_ref.shape[0] // width)
+            @pl.loop(0, up2_ref.shape[0] // width, unroll=True)
             def _(t):
                 tile = pl.ds(pl.multiple_of(t * width, width), width)
                 act = jax.nn.gelu(dot_t(perm1[k], up2p[tile, :]), approximate=True)

time: 132 us -> 131 us (level)
  no operation moved by 1% of the time
where the time goes in v7:
time: 131 us
  Pallas kernels  127 us (97%)
  local copies, waits for them, and re-layouts  3.16 us (2%)
    pallas_call x1, Pallas kernels, fused_layer(): pl.pallas_call(functools.partial(layer_kernel, n_seq, n_chan), out_shape=...  127 us
    unnamed x1, local copies, waits for them, and re-layouts  3.16 us

profile of v7, /device:TPU:29, one launch (start us, length us, event | category | flops | bytes accessed | tf_op | source)
XLA Modules:
  0.0 130.6 jit_solution(13467619024791420789)
XLA Ops:
  0.0 127.4 %shard_map.91 = bf16[2,8,2,16,2048]{4,3,2,1,0:T(8,128)(2,1)} custom-call(bf16[2,4,8,2,16,512]{5,4,3,2,1,0:T(8,128)(2,1)} %bitcast.10, bf16[4,256,256]{2,1,0:T(8,128)(2,1)} %mix1_ref.1, bf16[2,512,32]{2,1,0:T(8,128)(2,1)} %bitcast.15, f32[1,512]{1,0:T(1,128)} %bitcast.16, f32[1,512]{1,0:T(1,128)} %bitcast.17, bf16[512,512]{1,0:T(8,128)(2,1)} %bitcast.13, ...), custom_call_target="tpu_custom_call" | custom-call | tf_op jit(solution)/shard_map/pallas_call | solution.py:350
  127.4 3.2 %copy.11 = bf16[2,256,2048]{2,1,0:T(8,128)(2,1)} copy(bf16[2,256,2048]{2,1,0:T(8,128)(2,1)} %bitcast.9) | data formatting | bytes 4194304
